TPU v7x, 32 devices: a whole 2x2x4 slice. The times are simulated.
32 devices in a mesh: row: 4 (over y, x), col: 8 (over z, core).
Axes of the slice: x: 2, y: 2, z: 4, core: 2. Of those that a mesh axis runs over, the one named last changes fastest.
Arguments:
- inverse_block: float32 [12288, 12288], P('row', 'col'), may hold values from -6 to 6
- factor_panel: float32 [3, 12288, 256], P(None, ('row', 'col')), may hold values from -0.0546875 to 0.0546875
- diag_inverse: float32 [3, 256, 256], P(None, 'row'), may hold values from -6 to 6
- block_lists: int32 [3, 48], replicated, may hold values from 0 to 47, as said below
- list_counts: int32 [3], replicated, may hold values from 6 to 48, as said below
Outputs:
- solved: float32 [3, 12288, 256], P(None, ('row', 'col'))
- diag_block: float32 [3, 256, 256], P(None, 'row')
Inputs may be any that keep to these rules, and one draw needn't show every extreme that they name: `block_lists`: row k is an ordering of all 48 ancestor blocks; its first list_counts[k] entries are the blocks listed for supernode k. `list_counts`: one supernode lists all 48 blocks and one lists 48 // 8 of them.
All inputs are finite; a program needn't handle non-finite values.
Results may differ from a plain program's by a relative error of at most 0.000071.
Values sent between devices are 32-bit elements; how exact they have to be, the bound alone decides.
A program may use at most 64 MiB of HBM per device.

v0:
```python
import jax
import jax.numpy as jnp
from jax import lax
from jax.sharding import PartitionSpec as P

NA = 12288
BLK = 256


def broadcast(block, axis, source):
    block = jnp.where(lax.axis_index(axis) == source, block, jnp.zeros_like(block))
    return lax.psum(block, axis)


def listed_table(block_lists, list_counts, nblocks):
    entries = jnp.arange(block_lists.shape[1], dtype=jnp.int32)
    active = entries[None, :] < list_counts[:, None]
    hits = (
        block_lists[:, :, None] == jnp.arange(nblocks, dtype=jnp.int32)[None, None, :]
    ) & active[:, :, None]
    return jnp.any(hits, axis=1).astype(jnp.float32)


def rows_mask(table, first_row, count):
    global_rows = first_row + jnp.arange(count, dtype=jnp.int32)
    onehot = (
        (global_rows // BLK)[:, None] == jnp.arange(table.shape[1], dtype=jnp.int32)[None, :]
    ).astype(jnp.float32)
    return jnp.dot(table, onehot.T, precision=lax.Precision.HIGHEST)


def apply_block(inverse_block, panels):
    results = []
    for member in range(panels.shape[0]):
        panel_rows = panels[member]
        summed = jnp.dot(inverse_block, panel_rows, precision=lax.Precision.HIGHEST)
        results.append(summed)
    return jnp.stack(results)


def per_device(inverse_block, factor_panel, diag_inverse, block_lists, list_counts):
    n_row = lax.axis_size("row")
    n_col = lax.axis_size("col")
    row_id = lax.axis_index("row")
    col_id = lax.axis_index("col")
    local_rows = factor_panel.shape[1]
    span_row = inverse_block.shape[0]
    span_col = inverse_block.shape[1]
    table = listed_table(block_lists, list_counts, NA // BLK)
    mask_local = rows_mask(table, (row_id * n_col + col_id) * local_rows, local_rows)
    mask_range = rows_mask(table, row_id * span_row, span_row)
    group_ratio = n_col // n_row
    source_row = col_id // group_ratio
    start_col = col_id % group_ratio * span_col
    gathered = lax.all_gather(factor_panel, "col", axis=1, tiled=True)
    masked_range = gathered * mask_range[:, :, None]
    piece = lax.dynamic_slice_in_dim(masked_range, start_col, span_col, 1)
    columns = broadcast(piece, "row", source_row)
    partial_value = apply_block(inverse_block, columns) * mask_range[:, :, None]
    solved = -lax.psum_scatter(partial_value, "col", scatter_dimension=1, tiled=True)
    masked_local = factor_panel * mask_local[:, :, None]
    terms = jnp.einsum("knw,knv->kwv", masked_local, solved, precision=lax.Precision.HIGHEST)
    shares = lax.psum_scatter(terms, "row", scatter_dimension=1, tiled=True)
    diag_block = diag_inverse - lax.psum(shares, "col")
    return (solved, diag_block)


def solution(mesh):
    placed = (P("row", "col"), P(None, ("row", "col"), None), P(None, "row", None), P(), P())
    return jax.shard_map(
        per_device,
        mesh=mesh,
        in_specs=placed,
        out_specs=(P(None, ("row", "col"), None), P(None, "row", None)),
        check_vma=False,
    )
```

profile of v0, /device:TPU:0, one launch (start us, length us, event | category | flops | bytes accessed | tf_op | source)
XLA Modules:
  0.0 475.3 jit_solution(13311766748399240605)
XLA Ops:
  7.2 0.0 all-gather.2.cloned.1.call-start
  7.2 2.7 copy.11
  9.9 0.0 all-gather.2.cloned.1.call-update
  9.9 0.0 all-reduce.3.cloned.1.call-start
  10.0 0.7 iota_compare_fusion.5
  10.7 0.8 fusion.9
  11.5 1.6 fusion.1
  13.1 90.5 %all-gather.2.cloned.1.call-done = f32[3,3072,256]{1,2,0:T(8,128)} async-done(((f32[3,384,256]{1,2,0:T(8,128)}), f32[3,3072,256]{1,2,0:T(8,128)}) %all-gather.2.cloned.1.call-update) | async-done | bytes 9437200 | tf_op jit(solution)/shard_map/all_gather | solution.py:55
  103.7 5.1 %fusion = f32[3,1536,256]{1,2,0:T(8,128)} fusion(f32[3,3072,256]{1,2,0:T(8,128)} %all-gather.2.cloned.1.call-done, s32[]{:T(128)S(6)} %select_n.44, f32[3,1536]{1,0:T(4,128)S(1)} %constant_dynamic-slice_fusion, pred[]{:T(512)S(6)} %eq.21), kind=kLoop, calls=%fused_computation.2 | loop fusion | flops 2359296 | bytes 9455621 | tf_op jit(solution)/shard_map/jit(_where)/select_n | solution.py:11
  108.8 0.0 all-reduce.3.cloned.1.call-update
  108.8 0.0 reduce-scatter.3.cloned.1.call-start
  108.9 111.0 %all-reduce.3.cloned.1.call-done = f32[3,1536,256]{1,2,0:T(8,128)} async-done(((f32[3,1536,256]{1,2,0:T(8,128)}), f32[3,1536,256]{1,2,0:T(8,128)}) %all-reduce.3.cloned.1.call-update) | async-done | bytes 4718608 | tf_op jit(solution)/shard_map/psum | solution.py:12
  219.9 0.0 copy-start
  219.9 0.0 slice-start
  219.9 0.0 slice-start.1
  219.9 0.0 slice-start.2
  219.9 19.8 %convolution_bitcast_fusion = f32[1,3072,256]{1,2,0:T(8,128)S(1)} fusion(f32[3072,1536]{1,0:T(8,128)} %param.5, f32[3,1536,256]{1,2,0:T(8,128)} %all-reduce.3.cloned.1.call-done), kind=kOutput, calls=%fused_computation.3 | convolution fusion | flops 14495514624 | bytes 23592960 | tf_op jit(solution)/shard_map/dot_general | solution.py:36
  239.7 0.0 copy-done
  239.7 0.0 slice-start.3
  239.7 0.0 slice-start.4
  239.7 19.4 %convolution_bitcast_fusion.1 = f32[1,3072,256]{1,2,0:T(8,128)S(1)} fusion(f32[3072,1536]{1,0:T(8,128)} %param.5, f32[3,1536,256]{1,2,0:T(8,128)S(1)} %copy-done), kind=kOutput, calls=%fused_computation.4 | convolution fusion | flops 14495514624 | bytes 23592960 | tf_op jit(solution)/shard_map/dot_general | solution.py:36
  259.1 0.0 slice-done
  259.1 0.0 slice-done.1
  259.2 0.0 slice-done.2
  259.2 0.0 slice-done.3
  259.2 0.0 slice-done.4
  259.2 18.2 %convolution_bitcast_fusion.2 = f32[1,3072,256]{1,2,0:T(8,128)S(1)} fusion(f32[3072,1536]{1,0:T(8,128)S(1)} %bitcast.27, f32[3,1536,256]{1,2,0:T(8,128)} %all-reduce.3.cloned.1.call-done), kind=kOutput, calls=%fused_computation.5 | convolution fusion | flops 14495514624 | bytes 23592960 | tf_op jit(solution)/shard_map/dot_general | solution.py:36
  277.4 4.2 maximum_multiply_fusion
  281.6 0.0 copy-start.1
  281.6 0.0 reduce-scatter.3.cloned.1.call-update
  281.6 0.0 copy-start.3
  281.6 0.0 reduce-scatter.5.cloned.1.call-start
  281.7 0.2 fusion.6
  281.9 99.4 %reduce-scatter.3.cloned.1.call-done = f32[3,384,256]{1,2,0:T(8,128)} async-done(((f32[3,3072,256]{1,2,0:T(8,128)}), f32[3,384,256]{1,2,0:T(8,128)}) %reduce-scatter.3.cloned.1.call-update) | async-done | bytes 1179664 | tf_op jit(solution)/shard_map/reduce_scatter | solution.py:60
  381.3 0.0 copy-done.1
  381.3 0.0 copy-start.2
  381.3 4.5 fusion.2
  385.7 0.0 reduce-scatter.5.cloned.1.call-update
  385.8 0.0 all-reduce.5.cloned.1.call-start
  385.8 24.5 %reduce-scatter.5.cloned.1.call-done = f32[3,64,256]{2,1,0:T(8,128)} async-done(((f32[3,256,256]{2,1,0:T(8,128)}), f32[3,64,256]{2,1,0:T(8,128)}) %reduce-scatter.5.cloned.1.call-update) | async-done | bytes 196624 | tf_op jit(solution)/shard_map/reduce_scatter | solution.py:63
  410.4 0.0 all-reduce.5.cloned.1.call-update
  410.4 0.0 copy-done.2
  410.4 0.1 neg.3
  410.5 1.4 copy.14
  411.9 55.3 %all-reduce.5.cloned.1.call-done = f32[3,64,256]{2,1,0:T(8,128)} async-done(((f32[3,64,256]{2,1,0:T(8,128)}), f32[3,64,256]{2,1,0:T(8,128)}) %all-reduce.5.cloned.1.call-update) | async-done | bytes 196624 | tf_op jit(solution)/shard_map/psum | solution.py:64
  467.1 0.0 copy-done.3
  467.1 1.6 sub.22
  (4 shorter events, 0.0 us)
Async XLA Ops:
  7.2 96.5 %all-gather.2.cloned.1.call-start = ((), (), s32[]{:S(2)}) async-start(), calls=%async_computation.2 | async-start | bytes 10616832 | tf_op jit(solution)/shard_map/all_gather | solution.py:55
  9.9 210.0 %all-reduce.3.cloned.1.call-start = ((), (), s32[]{:S(2)}) async-start(), calls=%async_computation.3 | async-start | bytes 9437184 | tf_op jit(solution)/shard_map/psum | solution.py:12
  108.8 272.4 %reduce-scatter.3.cloned.1.call-start = ((), (), s32[]{:S(2)}) async-start(), calls=%async_computation.4 | async-start | bytes 10616832 | tf_op jit(solution)/shard_map/reduce_scatter | solution.py:60
  219.9 19.8 %copy-start = (f32[3,1536,256]{1,2,0:T(8,128)S(1)}, f32[3,1536,256]{1,2,0:T(8,128)}, u32[]{:S(2)}) copy-start(f32[3,1536,256]{1,2,0:T(8,128)} %all-reduce.3.cloned.1.call-done) | copy-start | bytes 14155780
  219.9 39.3 %slice-start = ((s8[18874368]{0:T(1024)(128)(4,1)}), s8[4194304]{0:T(1024)(128)(4,1)S(1)}, s32[]{:S(2)}) async-start(s8[18874368]{0:T(1024)(128)(4,1)} %bitcast.26), calls=%async_computation.7 | async-start | bytes 8388608
  219.9 39.3 %slice-start.1 = ((s8[18874368]{0:T(1024)(128)(4,1)}), s8[4194304]{0:T(1024)(128)(4,1)S(1)}, s32[]{:S(2)}) async-start(s8[18874368]{0:T(1024)(128)(4,1)} %bitcast.26), calls=%async_computation.8 | async-start | bytes 8388608
  219.9 39.3 %slice-start.2 = ((s8[18874368]{0:T(1024)(128)(4,1)}), s8[4194304]{0:T(1024)(128)(4,1)S(1)}, s32[]{:S(2)}) async-start(s8[18874368]{0:T(1024)(128)(4,1)} %bitcast.26), calls=%async_computation.9 | async-start | bytes 8388608
  239.7 19.5 %slice-start.3 = ((s8[18874368]{0:T(1024)(128)(4,1)}), s8[4194304]{0:T(1024)(128)(4,1)S(1)}, s32[]{:S(2)}) async-start(s8[18874368]{0:T(1024)(128)(4,1)} %bitcast.26), calls=%async_computation.10 | async-start | bytes 8388608
  239.7 19.5 %slice-start.4 = ((s8[18874368]{0:T(1024)(128)(4,1)}), s8[2097152]{0:T(1024)(128)(4,1)S(1)}, s32[]{:S(2)}) async-start(s8[18874368]{0:T(1024)(128)(4,1)} %bitcast.26), calls=%async_computation.11 | async-start | bytes 4194304
  281.6 99.7 %copy-start.1 = (f32[3,384,256]{2,1,0:T(8,128)S(1)}, f32[3,384,256]{2,1,0:T(8,128)}, u32[]{:S(2)}) copy-start(f32[3,384,256]{2,1,0:T(8,128)} %param.6) | copy-start | bytes 3538948
  281.6 185.6 %copy-start.3 = (f32[3,64,256]{2,1,0:T(8,128)S(1)}, f32[3,64,256]{2,1,0:T(8,128)}, u32[]{:S(2)}) copy-start(f32[3,64,256]{2,1,0:T(8,128)} %param.7) | copy-start | bytes 589828
  281.6 128.8 %reduce-scatter.5.cloned.1.call-start = ((), (), s32[]{:S(2)}) async-start(), calls=%async_computation.5 | async-start | bytes 983040 | tf_op jit(solution)/shard_map/reduce_scatter | solution.py:63
  381.3 29.1 %copy-start.2 = (f32[3,384,256]{1,2,0:T(8,128)S(1)}, f32[3,384,256]{1,2,0:T(8,128)}, u32[]{:S(2)}) copy-start(f32[3,384,256]{1,2,0:T(8,128)} %reduce-scatter.3.cloned.1.call-done) | copy-start | bytes 3538948
  385.8 81.4 %all-reduce.5.cloned.1.call-start = ((), (), s32[]{:S(2)}) async-start(), calls=%async_computation.6 | async-start | bytes 393216 | tf_op jit(solution)/shard_map/psum | solution.py:64
Sparse Core Ops, SparseCore 0:
  10.2 93.4 all-gather.1
  108.9 110.8 all-reduce.2
  281.7 99.5 reduce-scatter.2
  385.9 24.4 reduce-scatter.4
  412.5 54.5 all-reduce.4
where the time goes:
time: 476 us; the launch traced here: 475 us
  waiting for transfers between devices  381 us (80%)
  matrix products  63.7 us (13%)
  between operations  14 us (3%)
  other arithmetic  12.6 us (3%)
    psum x1, waiting for transfers between devices, broadcast(): return lax.psum(block, axis)  111 us
    reduce_scatter x1, waiting for transfers between devices, per_device(): lax.psum_scatter(partial_value, 'col', scatter_dimension=1, tiled=True)  99.4 us
    all_gather x1, waiting for transfers between devices, per_device(): gathered = lax.all_gather(factor_panel, 'col', axis=1, tiled=True)  90.5 us
    dot_general x3, matrix products, apply_block(): summed = jnp.dot(inverse_block, panel_rows, precision=lax.Precision.HIGHEST)  57.4 us
    psum x1, waiting for transfers between devices, per_device(): diag_block = diag_inverse - lax.psum(shares, 'col')  55.3 us
    reduce_scatter x1, waiting for transfers between devices, per_device(): shares = lax.psum_scatter(terms, 'row', scatter_dimension=1, tiled=True)  24.5 us
  transfers between devices with their start and end apart: 5, of which 5 were waited for; matrix products, arithmetic and copies ran while one was open for 1% of the time, Pallas kernels for 0%

commit v1 on v0

v1 whole, which is shorter than its diff:
```python
import functools

import jax
import jax.numpy as jnp
from jax import lax
from jax.experimental import pallas as pl
from jax.experimental.pallas import tpu as pltpu
from jax.sharding import PartitionSpec as P

MESH = pl.DeviceIdType.MESH


def listed_table(block_lists, list_counts, nblocks):
    entries = jnp.arange(block_lists.shape[1], dtype=jnp.int32)
    active = entries[None, :] < list_counts[:, None]
    hits = (
        block_lists[:, :, None] == jnp.arange(nblocks, dtype=jnp.int32)[None, None, :]
    ) & active[:, :, None]
    return jnp.any(hits, axis=1).astype(jnp.float32)


def rows_mask(table, first_row, count, block):
    global_rows = first_row + jnp.arange(count, dtype=jnp.int32)
    onehot = (global_rows // block)[:, None] == jnp.arange(table.shape[1], dtype=jnp.int32)[None, :]
    return jnp.any(onehot[None] & (table > 0)[:, None, :], axis=2)


def sum_kernel(n_row, n_col, terms, out, recv, send1, recv1, send2, recv2):
    n = n_row * n_col
    row, col = lax.axis_index("row"), lax.axis_index("col")
    me = row * n_col + col

    barrier = pltpu.get_barrier_semaphore()

    def greet(d, carry):
        other = lax.rem(me + d, n)
        pl.semaphore_signal(
            barrier, inc=1, device_id=(other // n_col, lax.rem(other, n_col)), device_id_type=MESH
        )
        return carry

    lax.fori_loop(1, n, greet, 0)
    pl.semaphore_wait(barrier, n - 1)

    def spread(other):
        to_row, to_col = other // n_col, lax.rem(other, n_col)
        return pltpu.make_async_remote_copy(
            src_ref=terms.at[to_row, to_col],
            dst_ref=recv.at[me],
            send_sem=send1.at[other],
            recv_sem=recv1.at[me],
            device_id=(to_row, to_col),
            device_id_type=MESH,
        )

    def arrive(other):
        return pltpu.make_async_remote_copy(
            src_ref=terms.at[row, col],
            dst_ref=recv.at[other],
            send_sem=send1.at[other],
            recv_sem=recv1.at[other],
            device_id=(row, col),
            device_id_type=MESH,
        )

    def start1(d, carry):
        spread(lax.rem(me + d, n)).start()
        return carry

    lax.fori_loop(1, n, start1, 0)

    def add(d, total):
        other = lax.rem(me + n - d, n)
        arrive(other).wait_recv()
        return total + recv[other]

    total = lax.fori_loop(1, n, add, terms[row, col])
    out[col] = total

    def share(to_col):
        return pltpu.make_async_remote_copy(
            src_ref=out.at[col],
            dst_ref=out.at[col],
            send_sem=send2.at[to_col],
            recv_sem=recv2.at[col],
            device_id=(row, to_col),
            device_id_type=MESH,
        )

    def shared(from_col):
        return pltpu.make_async_remote_copy(
            src_ref=out.at[from_col],
            dst_ref=out.at[from_col],
            send_sem=send2.at[from_col],
            recv_sem=recv2.at[from_col],
            device_id=(row, from_col),
            device_id_type=MESH,
        )

    def start2(d, carry):
        share(lax.rem(col + d, n_col)).start()
        return carry

    lax.fori_loop(1, n_col, start2, 0)

    def end1(d, carry):
        spread(lax.rem(me + d, n)).wait_send()
        return carry

    lax.fori_loop(1, n, end1, 0)

    def end2(d, carry):
        shared(lax.rem(col + n_col - d, n_col)).wait_recv()
        share(lax.rem(col + d, n_col)).wait_send()
        return carry

    lax.fori_loop(1, n_col, end2, 0)


def sum_terms(terms, n_row, n_col):
    members, width, _ = terms.shape
    n = n_row * n_col
    lanes = 128
    depth = members * width * width // (n * lanes)
    terms = terms.reshape(members, n_row, width // n_row, width).transpose(1, 0, 2, 3)
    terms = terms.reshape(n_row, n_col, depth, lanes)
    total = pl.pallas_call(
        functools.partial(sum_kernel, n_row, n_col),
        out_shape=jax.ShapeDtypeStruct((n_col, depth, lanes), jnp.float32),
        in_specs=[pl.BlockSpec(memory_space=pltpu.VMEM)],
        out_specs=pl.BlockSpec(memory_space=pltpu.VMEM),
        scratch_shapes=[
            pltpu.VMEM((n, depth, lanes), jnp.float32),
            pltpu.SemaphoreType.DMA((n,)),
            pltpu.SemaphoreType.DMA((n,)),
            pltpu.SemaphoreType.DMA((n_col,)),
            pltpu.SemaphoreType.DMA((n_col,)),
        ],
        compiler_params=pltpu.CompilerParams(collective_id=1, has_side_effects=True),
        name="sum_terms",
    )(terms)
    return total.reshape(members, width // n_row, width)


def per_device(n_row, n_col, inverse_block, factor_panel, diag_inverse, block_lists, list_counts):
    row_id = lax.axis_index("row")
    col_id = lax.axis_index("col")
    members, local_rows, _ = factor_panel.shape
    nblocks = block_lists.shape[1]
    block = local_rows * n_row * n_col // nblocks
    n = n_row * n_col
    table = listed_table(block_lists, list_counts, nblocks)
    mask_local = rows_mask(table, (row_id * n_col + col_id) * local_rows, local_rows, block)
    masked_local = jnp.where(mask_local[:, :, None], factor_panel, 0.0)
    perm = [(p, (p % n_row) * n_col + p // n_row) for p in range(n)]
    solved = []
    for k in range(members):
        piece = lax.ppermute(masked_local[k], ("row", "col"), perm)
        columns = lax.all_gather(piece, "row", axis=0, tiled=True)
        product = jnp.dot(inverse_block, columns, precision=lax.Precision.HIGH)
        solved.append(lax.psum_scatter(product, "col", scatter_dimension=0, tiled=True))
    solved = jnp.where(mask_local[:, :, None], -jnp.stack(solved), 0.0)
    terms = jnp.einsum("knw,knv->kwv", masked_local, solved, precision=lax.Precision.HIGHEST)
    return (solved, diag_inverse - sum_terms(terms, n_row, n_col))


def solution(mesh):
    n_row, n_col = mesh.shape["row"], mesh.shape["col"]
    placed = (P("row", "col"), P(None, ("row", "col"), None), P(None, "row", None), P(), P())
    return jax.shard_map(
        functools.partial(per_device, n_row, n_col),
        mesh=mesh,
        in_specs=placed,
        out_specs=(P(None, ("row", "col"), None), P(None, "row", None)),
        check_vma=False,
    )
```

time: 476 us -> 333 us (0.70)
  waiting for transfers between devices: 381 us -> 236 us
  Pallas kernels: 0 us -> 28.6 us
  matrix products: 63.7 us -> 41.1 us
  other arithmetic: 12.6 us -> 3.79 us
    psum x2 -> x0, waiting for transfers between devices: 166 us -> none  [the longest x1 111 us: broadcast(): return lax.psum(block, axis)]
    all_gather x1 -> x3, waiting for transfers between devices: 90.5 us -> 123 us  [per_device(): columns = lax.all_gather(piece, 'row', axis=0, tiled=True)]
    pallas_call x0 -> x1, Pallas kernels: none -> 28.6 us  [sum_terms(): pl.pallas_call(functools.partial(sum_kernel, n_row, n_col), out_shape=jax...]
    dot_general x5 -> x3, matrix products: 59.2 us -> 39.6 us  [per_device(): product = jnp.dot(inverse_block, columns, precision=lax.Precision.HIGH)]
    reduce_scatter x2 -> x3, waiting for transfers between devices: 124 us -> 113 us  [per_device(): lax.psum_scatter(product, 'col', scatter_dimension=0, tiled=True)]
  transfers between devices with their start and end apart: 5 -> 9, of which waited for: 5 -> 6; matrix products, arithmetic and copies ran while one was open for 1% -> 12% of each run, Pallas kernels for 0% -> 0%
where the time goes in v1:
time: 333 us
  waiting for transfers between devices  236 us (71%)
  matrix products  41.1 us (12%)
  Pallas kernels  28.6 us (9%)
  between operations  14.3 us (4%)
  local copies, waits for them, and re-layouts  7.33 us (2%)
  other arithmetic  3.79 us (1%)
    all_gather x3, waiting for transfers between devices, per_device(): columns = lax.all_gather(piece, 'row', axis=0, tiled=True)  123 us
    reduce_scatter x3, waiting for transfers between devices, per_device(): lax.psum_scatter(product, 'col', scatter_dimension=0, tiled=True)  113 us
    dot_general x3, matrix products, per_device(): product = jnp.dot(inverse_block, columns, precision=lax.Precision.HIGH)  39.6 us
    pallas_call x1, Pallas kernels, sum_terms(): pl.pallas_call(functools.partial(sum_kernel, n_row, n_col), out_shape=jax...  28.6 us
  transfers between devices with their start and end apart: 9, of which 6 were waited for; matrix products, arithmetic and copies ran while one was open for 12% of the time, Pallas kernels for 0%

profile of v1, /device:TPU:0, one launch (start us, length us, event | category | flops | bytes accessed | tf_op | source)
XLA Modules:
  0.0 333.2 jit_solution(17510599399551811880)
XLA Ops:
  7.2 0.0 all-gather.4.cloned.1.call-start
  7.3 0.7 iota_compare_fusion.2
  8.0 0.8 fusion.2
  8.8 1.6 copy.11
  10.4 0.1 and_reduce_fusion
  10.5 0.1 broadcast_select_fusion
  10.6 0.1 slice_bitcast_fusion.2
  10.7 0.7 collective-permute-start
  11.4 0.0 collective-permute-done
  11.4 0.0 copy-start
  11.4 0.7 copy-done
  12.2 0.0 all-gather.4.cloned.1.call-update
  12.2 0.0 all-gather.6.cloned.1.call-start
  12.3 0.7 collective-permute-start.1
  12.9 0.0 collective-permute-done.1
  13.0 0.0 copy-start.1
  13.0 0.7 copy-done.1
  13.7 0.0 all-gather.6.cloned.1.call-update
  13.7 0.0 all-gather.8.cloned.1.call-start
  13.8 0.7 collective-permute-start.2
  14.5 0.0 collective-permute-done.2
  14.5 0.0 copy-start.2
  14.5 0.7 copy-done.2
  15.2 0.0 all-gather.8.cloned.1.call-update
  15.3 0.0 reduce-scatter.4.cloned.1.call-start
  15.3 75.9 %all-gather.4.cloned.1.call-done = f32[1536,256]{0,1:T(8,128)} async-done(((f32[384,256]{0,1:T(8,128)}), f32[1536,256]{0,1:T(8,128)}) %all-gather.4.cloned.1.call-update) | async-done | bytes 1572880 | tf_op jit(solution)/shard_map/all_gather | solution.py:159
  91.2 13.2 %convolution_bitcast_fusion.2 = f32[3072,256]{0,1:T(8,128)} fusion(f32[1536,256]{0,1:T(8,128)} %all-gather.4.cloned.1.call-done, f32[3072,1536]{1,0:T(8,128)} %param.5), kind=kOutput, calls=%fused_computation.2 | convolution fusion | flops 7247757312 | bytes 23592960 | tf_op jit(solution)/shard_map/dot_general | solution.py:160
  104.4 0.0 reduce-scatter.4.cloned.1.call-update
  104.4 0.0 reduce-scatter.6.cloned.1.call-start
  104.4 27.1 %all-gather.6.cloned.1.call-done = f32[1536,256]{0,1:T(8,128)} async-done(((f32[384,256]{0,1:T(8,128)}), f32[1536,256]{0,1:T(8,128)}) %all-gather.6.cloned.1.call-update) | async-done | bytes 1572880 | tf_op jit(solution)/shard_map/all_gather | solution.py:159
  131.5 13.2 %convolution_bitcast_fusion.1 = f32[3072,256]{0,1:T(8,128)} fusion(f32[1536,256]{0,1:T(8,128)} %all-gather.6.cloned.1.call-done, f32[3072,1536]{1,0:T(8,128)} %param.5), kind=kOutput, calls=%fused_computation.1 | convolution fusion | flops 7247757312 | bytes 23592960 | tf_op jit(solution)/shard_map/dot_general | solution.py:160
  144.7 0.0 reduce-scatter.6.cloned.1.call-update
  144.7 0.2 reduce-scatter.8.cloned.1.call-start
  145.0 20.0 %all-gather.8.cloned.1.call-done = f32[1536,256]{0,1:T(8,128)} async-done(((f32[384,256]{0,1:T(8,128)}), f32[1536,256]{0,1:T(8,128)}) %all-gather.8.cloned.1.call-update) | async-done | bytes 1572880 | tf_op jit(solution)/shard_map/all_gather | solution.py:159
  165.0 13.2 %convolution_bitcast_fusion = f32[3072,256]{0,1:T(8,128)} fusion(f32[1536,256]{0,1:T(8,128)} %all-gather.8.cloned.1.call-done, f32[3072,1536]{1,0:T(8,128)} %param.5), kind=kOutput, calls=%fused_computation | convolution fusion | flops 7247757312 | bytes 23592960 | tf_op jit(solution)/shard_map/dot_general | solution.py:160
  178.1 0.0 reduce-scatter.8.cloned.1.call-update
  178.2 29.3 %reduce-scatter.4.cloned.1.call-done = f32[384,256]{0,1:T(8,128)} async-done(((f32[3072,256]{0,1:T(8,128)}), f32[384,256]{0,1:T(8,128)}) %reduce-scatter.4.cloned.1.call-update) | async-done | bytes 393232 | tf_op jit(solution)/shard_map/reduce_scatter | solution.py:161
  207.5 41.6 %reduce-scatter.6.cloned.1.call-done = f32[384,256]{0,1:T(8,128)} async-done(((f32[3072,256]{0,1:T(8,128)}), f32[384,256]{0,1:T(8,128)}) %reduce-scatter.6.cloned.1.call-update) | async-done | bytes 393232 | tf_op jit(solution)/shard_map/reduce_scatter | solution.py:161
  249.1 41.6 %reduce-scatter.8.cloned.1.call-done = f32[384,256]{0,1:T(8,128)} async-done(((f32[3072,256]{0,1:T(8,128)}), f32[384,256]{0,1:T(8,128)}) %reduce-scatter.8.cloned.1.call-update) | async-done | bytes 393232 | tf_op jit(solution)/shard_map/reduce_scatter | solution.py:161
  290.7 1.3 fusion
  292.0 1.5 fusion.6
  293.5 1.4 copy.14
  294.9 0.1 copy.17
  295.0 0.0 copy-start.3
  295.0 0.9 reshape.79.terms
  296.0 28.6 %sum_terms.1 = f32[8,48,128]{2,1,0:T(8,128)} custom-call(f32[4,8,48,128]{3,2,1,0:T(8,128)} %reshape.79.terms), custom_call_target="tpu_custom_call" | custom-call | tf_op jit(solution)/shard_map/sum_terms/pallas_call | solution.py:127
  324.6 1.0 reshape.80
  325.6 0.0 copy-done.3
  325.6 0.7 sub.10
  (3 shorter events, 0.0 us)
Async XLA Ops:
  7.2 84.0 %all-gather.4.cloned.1.call-start = ((), (), s32[]{:S(2)}) async-start(), calls=%async_computation.3 | async-start | bytes 1966080 | tf_op jit(solution)/shard_map/all_gather | solution.py:159
  10.7 0.7 collective-permute-start
  11.4 0.8 copy-start
  12.2 119.3 %all-gather.6.cloned.1.call-start = ((), (), s32[]{:S(2)}) async-start(), calls=%async_computation.5 | async-start | bytes 1966080 | tf_op jit(solution)/shard_map/all_gather | solution.py:159
  12.3 0.7 collective-permute-start.1
  13.0 0.7 copy-start.1
  13.7 151.2 %all-gather.8.cloned.1.call-start = ((), (), s32[]{:S(2)}) async-start(), calls=%async_computation.7 | async-start | bytes 1966080 | tf_op jit(solution)/shard_map/all_gather | solution.py:159
  13.8 0.7 collective-permute-start.2
  14.5 0.7 copy-start.2
  15.3 192.2 %reduce-scatter.4.cloned.1.call-start = ((), (), s32[]{:S(2)}) async-start(), calls=%async_computation.4 | async-start | bytes 3538944 | tf_op jit(solution)/shard_map/reduce_scatter | solution.py:161
  104.4 144.7 %reduce-scatter.6.cloned.1.call-start = ((), (), s32[]{:S(2)}) async-start(), calls=%async_computation.6 | async-start | bytes 3538944 | tf_op jit(solution)/shard_map/reduce_scatter | solution.py:161
  144.7 145.9 %reduce-scatter.8.cloned.1.call-start = ((), (), s32[]{:S(2)}) async-start(), calls=%async_computation.8 | async-start | bytes 3538944 | tf_op jit(solution)/shard_map/reduce_scatter | solution.py:161
  295.0 30.6 %copy-start.3 = (f32[3,64,256]{2,1,0:T(8,128)S(1)}, f32[3,64,256]{2,1,0:T(8,128)}, u32[]{:S(2)}) copy-start(f32[3,64,256]{2,1,0:T(8,128)} %param.7) | copy-start | bytes 589828
Sparse Core Ops, SparseCore 0:
  12.3 78.7 all-gather.3
  93.0 38.4 all-gather.5
  133.9 30.9 all-gather.7
  167.1 40.3 reduce-scatter.3
  209.6 39.4 reduce-scatter.5
  251.2 39.4 reduce-scatter.7

commit v2 on v1

--- a/solution.py
+++ b/solution.py
@@ -142,6 +142,286 @@
     return total.reshape(members, width // n_row, width)
 
 
+def product_kernel(n_row, n_col, s_ref, x_ref, out, hop, xc, xs, hi, lo, stage, part_sum, sib, run,
+                   load, s0, r0, s1, r1, s2, r2, s3, r3, s4, r4):
+    n = n_row * n_col
+    chips = n_col // 2
+    members, local_rows, _ = x_ref.shape
+    splits, part = xc.shape[2], xc.shape[3]
+    group = n_row // splits
+    row, col = lax.axis_index("row"), lax.axis_index("col")
+    me = row * n_col + col
+    chip, core = col // 2, lax.rem(col, 2)
+    member_i = lax.rem(col, n_row)
+    my_split = row // group
+    first_i = lax.rem(row, group) * splits
+    relay = lax.rem(row, group) == member_i // splits
+
+    barrier = pltpu.get_barrier_semaphore()
+
+    def greet(d, carry):
+        other = lax.rem(me + d, n)
+        pl.semaphore_signal(
+            barrier, inc=1, device_id=(other // n_col, lax.rem(other, n_col)), device_id_type=MESH
+        )
+        return carry
+
+    lax.fori_loop(1, n, greet, 0)
+    pl.semaphore_wait(barrier, n - 1)
+
+    def remote(src, dst, send, recv, to):
+        return pltpu.make_async_remote_copy(
+            src_ref=src, dst_ref=dst, send_sem=send, recv_sem=recv, device_id=to, device_id_type=MESH
+        )
+
+    def hop0(k, q):
+        to_row = q * group + member_i // splits
+        return to_row, remote(
+            x_ref.at[k, pl.ds(q * part, part)], hop.at[k, row], s0.at[k, q], r0.at[k, row], (to_row, col)
+        )
+
+    def hop1(k, from_row):
+        to_col = (from_row * n_col + col) // n_row
+        return to_col, remote(
+            hop.at[k, from_row],
+            xc.at[k, member_i, my_split],
+            s1.at[k, from_row],
+            r1.at[k, lax.rem(member_i, splits)],
+            (row, to_col),
+        )
+
+    def hop2(k, d):
+        to_row = lax.rem(row + d, n_row)
+        block = xc.at[k, pl.ds(first_i, splits), my_split]
+        return remote(block, block, s2.at[k, to_row], r2.at[k, row], (to_row, col))
+
+    for k in range(members):
+        for q in range(splits):
+            to_row, copy = hop0(k, q)
+            pl.when(to_row != row)(copy.start)
+
+    chunk = stage.shape[1]
+    chunks = s_ref.shape[0] // chunk
+
+    def fetch(i):
+        slot = lax.rem(i, 2)
+        return pltpu.make_async_copy(
+            s_ref.at[pl.ds(i * chunk, chunk)], stage.at[slot], load.at[slot]
+        )
+
+    fetch(0).start()
+
+    def split_rows(i, carry):
+        @pl.when(i + 1 < chunks)
+        def _():
+            fetch(i + 1).start()
+
+        fetch(i).wait()
+        value = stage[lax.rem(i, 2)]
+        upper = value.astype(jnp.bfloat16)
+        rows = pl.ds(pl.multiple_of(i * chunk, chunk), chunk)
+        hi[rows, :] = upper
+        lo[rows, :] = (value - upper.astype(jnp.float32)).astype(jnp.bfloat16)
+        return carry
+
+    third = chunks // 3
+    lax.fori_loop(0, third, split_rows, 0)
+
+    for k in range(members):
+
+        @pl.when(relay)
+        def _():
+            hop[k, row] = x_ref[k, pl.ds(pl.multiple_of(my_split * part, 8), part), :]
+            for d in range(1, n_row):
+                from_row = lax.rem(row + d, n_row)
+                remote(
+                    hop.at[k, from_row], hop.at[k, from_row], s0.at[k, 0], r0.at[k, from_row], (row, col)
+                ).wait_recv()
+            for from_row in range(n_row):
+                to_col, copy = hop1(k, from_row)
+                pl.when(to_col != col)(copy.start)
+
+                @pl.when(to_col == col)
+                def _():
+                    xc[k, member_i, my_split] = hop[k, from_row]
+
+    lax.fori_loop(third, 2 * third, split_rows, 0)
+
+    for k in range(members):
+        for s in range(splits):
+            from_col = lax.rem(col * n_row + first_i + s, n_col)
+            block = xc.at[k, first_i + s, my_split]
+
+            @pl.when(from_col != col)
+            def _():
+                remote(block, block, s1.at[k, 0], r1.at[k, s], (row, col)).wait_recv()
+
+        for d in range(1, n_row):
+            hop2(k, d).start()
+
+    lax.fori_loop(2 * third, chunks, split_rows, 0)
+
+    def sibling(k, t):
+        return remote(
+            part_sum.at[k, 2 * t + 1 - core], sib.at[k, t], s3.at[k, t], r3.at[k, t],
+            (row, 2 * chip + 1 - core),
+        )
+
+    width = x_ref.shape[2]
+
+    def multiply(k):
+        for d in range(1, n_row):
+            from_row = lax.rem(row + d, n_row)
+            block = xc.at[k, pl.ds(lax.rem(from_row, group) * splits, splits), from_row // group]
+            remote(block, block, s2.at[k, 0], r2.at[k, from_row], (row, col)).wait_recv()
+        for i in range(n_row):
+            value = xc[k, i].reshape(local_rows, width)
+            upper = value.astype(jnp.bfloat16)
+            rows = pl.ds(i * local_rows, local_rows)
+            xs[rows, :width] = upper
+            xs[rows, width:] = (value - upper.astype(jnp.float32)).astype(jnp.bfloat16)
+
+        def owner_rows(j, carry):
+            t = lax.rem(j, chips)
+            owner = 2 * t + lax.rem(core + 1 + j // chips, 2)
+            rows = pl.ds(pl.multiple_of(owner * local_rows, 16), local_rows)
+            both = jnp.dot(hi[rows, :], xs[...], preferred_element_type=jnp.float32)
+            rest = jnp.dot(lo[rows, :], xs[:, :width], preferred_element_type=jnp.float32)
+            part_sum[k, owner] = both[:, :width] + (both[:, width:] + rest)
+
+            @pl.when(j < chips)
+            def _():
+                sibling(k, t).start()
+
+            return carry
+
+        lax.fori_loop(0, n_col, owner_rows, 0)
+
+    def passed(k, t, slot, to_chip):
+        return remote(
+            part_sum.at[k, 2 * t + core], run.at[k, slot], s4.at[k, t], r4.at[k, slot],
+            (row, 2 * to_chip + core),
+        )
+
+    def arrived(k, slot):
+        return remote(
+            run.at[k, slot], run.at[k, slot], s4.at[k, 0], r4.at[k, slot], (row, col)
+        )
+
+    def forward(k):
+        for t in range(chips):
+            sibling(k, t).wait()
+            part_sum[k, 2 * t + core] += sib[k, t]
+        for j in range(chips - 1):
+            t = chips - 1 - j
+
+            @pl.when(chip < t)
+            def _():
+                @pl.when(chip > 0)
+                def _():
+                    arrived(k, t + 1).wait_recv()
+                    part_sum[k, 2 * t + core] += run[k, t + 1]
+
+                passed(k, t, t + 1, chip + 1).start()
+
+            @pl.when(chip > j)
+            def _():
+                @pl.when(chip < chips - 1)
+                def _():
+                    arrived(k, j).wait_recv()
+                    part_sum[k, 2 * j + core] += run[k, j]
+
+                passed(k, j, j, chip - 1).start()
+
+    def finish(k):
+        out[k] = part_sum[k, col]
+
+        @pl.when(chip > 0)
+        def _():
+            arrived(k, chip + 1).wait_recv()
+            out[k] += run[k, chip + 1]
+
+        @pl.when(chip < chips - 1)
+        def _():
+            arrived(k, chip).wait_recv()
+            out[k] += run[k, chip]
+
+    for k in range(members):
+        multiply(k)
+        if k > 0:
+            forward(k - 1)
+    forward(members - 1)
+    for k in range(members):
+        finish(k)
+
+    for k in range(members):
+        for q in range(splits):
+            to_row, copy = hop0(k, q)
+            pl.when(to_row != row)(copy.wait_send)
+
+        @pl.when(relay)
+        def _():
+            for from_row in range(n_row):
+                to_col, copy = hop1(k, from_row)
+                pl.when(to_col != col)(copy.wait_send)
+
+        for d in range(1, n_row):
+            hop2(k, d).wait_send()
+        for t in range(chips):
+
+            @pl.when(chip < t)
+            def _():
+                passed(k, t, t + 1, chip + 1).wait_send()
+
+            @pl.when(chip > t)
+            def _():
+                passed(k, t, t, chip - 1).wait_send()
+
+
+def product(inverse_block, masked_local, n_row, n_col):
+    members, local_rows, width = masked_local.shape
+    span_row, span_col = inverse_block.shape
+    chips = n_col // 2
+    splits = max(d for d in range(1, n_row + 1) if n_row % d == 0 and local_rows % (8 * d) == 0)
+    part = local_rows // splits
+    chunk = span_row // 24
+    f32, bf16, sem = jnp.float32, jnp.bfloat16, pltpu.SemaphoreType.DMA
+    scratch = [
+        ((members, n_row, part, width), f32),
+        ((members, n_row, splits, part, width), f32),
+        ((span_col, 2 * width), bf16),
+        ((span_row, span_col), bf16),
+        ((span_row, span_col), bf16),
+        ((2, chunk, span_col), f32),
+        ((members, n_col, local_rows, width), f32),
+        ((members, chips, local_rows, width), f32),
+        ((members, chips + 1, local_rows, width), f32),
+    ]
+    macs = members * span_row * span_col * width
+    return pl.pallas_call(
+        functools.partial(product_kernel, n_row, n_col),
+        out_shape=jax.ShapeDtypeStruct(masked_local.shape, f32),
+        in_specs=[pl.BlockSpec(memory_space=pl.ANY), pl.BlockSpec(memory_space=pltpu.VMEM)],
+        out_specs=pl.BlockSpec(memory_space=pltpu.VMEM),
+        scratch_shapes=[pltpu.VMEM(shape, kind) for shape, kind in scratch]
+        + [
+            sem((2,)),
+            sem((members, splits)), sem((members, n_row)),
+            sem((members, n_row)), sem((members, splits)),
+            sem((members, n_row)), sem((members, n_row)),
+            sem((members, chips)), sem((members, chips)),
+            sem((members, chips)), sem((members, chips + 1)),
+        ],
+        compiler_params=pltpu.CompilerParams(
+            collective_id=2, has_side_effects=True, vmem_limit_bytes=60 * 2**20
+        ),
+        cost_estimate=pl.CostEstimate(
+            flops=6 * macs, bytes_accessed=4 * span_row * span_col, transcendentals=0
+        ),
+        name="product",
+    )(inverse_block, masked_local)
+
+
 def per_device(n_row, n_col, inverse_block, factor_panel, diag_inverse, block_lists, list_counts):
     row_id = lax.axis_index("row")
     col_id = lax.axis_index("col")
@@ -152,14 +432,7 @@
     table = listed_table(block_lists, list_counts, nblocks)
     mask_local = rows_mask(table, (row_id * n_col + col_id) * local_rows, local_rows, block)
     masked_local = jnp.where(mask_local[:, :, None], factor_panel, 0.0)
-    perm = [(p, (p % n_row) * n_col + p // n_row) for p in range(n)]
-    solved = []
-    for k in range(members):
-        piece = lax.ppermute(masked_local[k], ("row", "col"), perm)
-        columns = lax.all_gather(piece, "row", axis=0, tiled=True)
-        product = jnp.dot(inverse_block, columns, precision=lax.Precision.HIGH)
-        solved.append(lax.psum_scatter(product, "col", scatter_dimension=0, tiled=True))
-    solved = jnp.where(mask_local[:, :, None], -jnp.stack(solved), 0.0)
+    solved = jnp.where(mask_local[:, :, None], -product(inverse_block, masked_local, n_row, n_col), 0.0)
     terms = jnp.einsum("knw,knv->kwv", masked_local, solved, precision=lax.Precision.HIGHEST)
     return (solved, diag_inverse - sum_terms(terms, n_row, n_col))
 

time: 333 us -> 204 us (0.61)
  waiting for transfers between devices: 236 us -> 0 us
  Pallas kernels: 28.6 us -> 192 us
  matrix products: 41.1 us -> 2.14 us
  between operations: 14.3 us -> 0.73 us
  local copies, waits for them, and re-layouts: 7.33 us -> 2.01 us
    pallas_call x0 -> x1, Pallas kernels: none -> 160 us  [product(): pl.pallas_call(functools.partial(product_kernel, n_row, n_col), out_shape...]
    all_gather x3 -> x0, waiting for transfers between devices: 123 us -> none  [per_device(): columns = lax.all_gather(piece, 'row', axis=0, tiled=True)]
    reduce_scatter x3 -> x0, waiting for transfers between devices: 113 us -> none  [per_device(): lax.psum_scatter(product, 'col', scatter_dimension=0, tiled=True)]
    dot_general x3 -> x0, matrix products: 39.6 us -> none  [per_device(): product = jnp.dot(inverse_block, columns, precision=lax.Precision.HIGH)]
    unnamed x10 -> x6, local copies, waits for them, and re-layouts: 5.25 us -> 0.04 us
    pallas_call x1, Pallas kernels: 28.6 us -> 32.2 us  [sum_terms(): pl.pallas_call(functools.partial(sum_kernel, n_row, n_col), out_shape=jax...]
  transfers between devices with their start and end apart: 9 -> 0, of which waited for: 6 -> 0; matrix products, arithmetic and copies ran while one was open for 12% -> 0% of each run, Pallas kernels for 0% -> 0%
where the time goes in v2:
time: 204 us; the launch traced here: 203 us
  Pallas kernels  192 us (94%)
  other arithmetic  6.46 us (3%)
  matrix products  2.14 us (1%)
    pallas_call x1, Pallas kernels, product(): pl.pallas_call(functools.partial(product_kernel, n_row, n_col), out_shape...  160 us
    pallas_call x1, Pallas kernels, sum_terms(): pl.pallas_call(functools.partial(sum_kernel, n_row, n_col), out_shape=jax...  32.2 us

profile of v2, /device:TPU:0, one launch (start us, length us, event | category | flops | bytes accessed | tf_op | source)
XLA Modules:
  0.0 203.3 jit_solution(3913975868221318428)
XLA Ops:
  0.6 0.7 iota_compare_fusion.2
  1.4 0.8 fusion.1
  2.2 0.1 and_reduce_fusion
  2.3 2.5 %broadcast_select_fusion.x_ref = f32[3,384,256]{2,1,0:T(8,128)} fusion(f32[3,384,256]{2,1,0:T(8,128)} %param.6, pred[3,384]{1,0:T(4,128)(4,1)S(1)} %and_reduce_fusion), kind=kLoop, calls=%fused_computation.2 | loop fusion | flops 294912 | bytes 2360448 | tf_op jit(solution)/shard_map/jit(_where)/select_n | solution.py:434
  4.8 159.8 %product.1 = f32[3,384,256]{2,1,0:T(8,128)} custom-call(f32[3072,1536]{1,0:T(8,128)} %s_ref.1, f32[3,384,256]{2,1,0:T(8,128)} %broadcast_select_fusion.x_ref), custom_call_target="tpu_custom_call" | custom-call | flops 21743271936 | bytes 18874368 | tf_op jit(solution)/shard_map/product/pallas_call | solution.py:401
  164.6 0.0 copy-start.1
  164.6 1.6 negate_select_fusion
  166.2 0.0 copy-done.1
  166.2 0.0 copy-start
  166.2 2.1 %fusion.5 = f32[3,256,256]{2,1,0:T(8,128)S(1)} fusion(f32[3,384,256]{2,1,0:T(8,128)S(1)} %copy-done.1, f32[3,384,256]{2,1,0:T(8,128)S(1)} %negate_select_fusion), kind=kOutput, calls=%fused_computation.19 | convolution fusion | flops 905969664 | bytes 3145728 | tf_op jit(solution)/shard_map/knw,knv->kwv/dot_general | solution.py:436
  168.4 0.0 copy-done
  168.4 0.1 copy.13
  168.5 0.0 copy-start.2
  168.5 0.9 reshape.79.terms
  169.4 32.2 %sum_terms.1 = f32[8,48,128]{2,1,0:T(8,128)} custom-call(f32[4,8,48,128]{3,2,1,0:T(8,128)} %reshape.79.terms), custom_call_target="tpu_custom_call" | custom-call | tf_op jit(solution)/shard_map/sum_terms/pallas_call | solution.py:127
  201.6 1.0 reshape.80
  202.6 0.0 copy-done.2
  202.6 0.7 sub.10
  (3 shorter events, 0.0 us)
Async XLA Ops:
  164.6 1.6 copy-start.1
  166.2 2.2 %copy-start = (f32[3,384,256]{2,1,0:T(8,128)}, f32[3,384,256]{2,1,0:T(8,128)S(1)}, u32[]{:S(2)}) copy-start(f32[3,384,256]{2,1,0:T(8,128)S(1)} %negate_select_fusion) | copy-start | bytes 3538948
  168.5 34.1 %copy-start.2 = (f32[3,64,256]{2,1,0:T(8,128)S(1)}, f32[3,64,256]{2,1,0:T(8,128)}, u32[]{:S(2)}) copy-start(f32[3,64,256]{2,1,0:T(8,128)} %param.7) | copy-start | bytes 589828

commit v3 on v2

--- a/solution.py
+++ b/solution.py
@@ -308,29 +308,35 @@
             run.at[k, slot], run.at[k, slot], s4.at[k, 0], r4.at[k, slot], (row, col)
         )
 
-    def forward(k):
+    def begin(k):
         for t in range(chips):
             sibling(k, t).wait()
             part_sum[k, 2 * t + core] += sib[k, t]
+
+        @pl.when(chip == 0)
+        def _():
+            for t in range(chips - 1, 0, -1):
+                passed(k, t, t + 1, chip + 1).start()
+
+        @pl.when(chip == chips - 1)
+        def _():
+            for t in range(chips - 1):
+                passed(k, t, t, chip - 1).start()
+
+    def forward(k):
         for j in range(chips - 1):
             t = chips - 1 - j
 
-            @pl.when(chip < t)
-            def _():
-                @pl.when(chip > 0)
-                def _():
-                    arrived(k, t + 1).wait_recv()
-                    part_sum[k, 2 * t + core] += run[k, t + 1]
-
+            @pl.when((chip < t) & (chip > 0))
+            def _():
+                arrived(k, t + 1).wait_recv()
+                part_sum[k, 2 * t + core] += run[k, t + 1]
                 passed(k, t, t + 1, chip + 1).start()
 
-            @pl.when(chip > j)
-            def _():
-                @pl.when(chip < chips - 1)
-                def _():
-                    arrived(k, j).wait_recv()
-                    part_sum[k, 2 * j + core] += run[k, j]
-
+            @pl.when((chip > j) & (chip < chips - 1))
+            def _():
+                arrived(k, j).wait_recv()
+                part_sum[k, 2 * j + core] += run[k, j]
                 passed(k, j, j, chip - 1).start()
 
     def finish(k):
@@ -348,6 +354,7 @@
 
     for k in range(members):
         multiply(k)
+        begin(k)
         if k > 0:
             forward(k - 1)
     forward(members - 1)

time: 204 us -> 204 us (level)
    pallas_call x1, Pallas kernels: 32.2 us -> 41 us  [sum_terms(): pl.pallas_call(functools.partial(sum_kernel, n_row, n_col), out_shape=jax...]
    pallas_call x1, Pallas kernels: 160 us -> 151 us  [product(): pl.pallas_call(functools.partial(product_kernel, n_row, n_col), out_shape...]
where the time goes in v3:
time: 204 us; the launch traced here: 203 us
  Pallas kernels  192 us (94%)
  other arithmetic  6.46 us (3%)
  matrix products  2.14 us (1%)
    pallas_call x1, Pallas kernels, product(): pl.pallas_call(functools.partial(product_kernel, n_row, n_col), out_shape...  151 us
    pallas_call x1, Pallas kernels, sum_terms(): pl.pallas_call(functools.partial(sum_kernel, n_row, n_col), out_shape=jax...  41 us

profile of v3, /device:TPU:0, one launch (start us, length us, event | category | flops | bytes accessed | tf_op | source)
XLA Modules:
  0.0 203.5 jit_solution(392425274884337105)
XLA Ops:
  0.6 0.7 iota_compare_fusion.2
  1.4 0.8 fusion.1
  2.2 0.1 and_reduce_fusion
  2.3 2.5 %broadcast_select_fusion.x_ref = f32[3,384,256]{2,1,0:T(8,128)} fusion(f32[3,384,256]{2,1,0:T(8,128)} %param.6, pred[3,384]{1,0:T(4,128)(4,1)S(1)} %and_reduce_fusion), kind=kLoop, calls=%fused_computation.2 | loop fusion | flops 294912 | bytes 2360448 | tf_op jit(solution)/shard_map/jit(_where)/select_n | solution.py:441
  4.8 151.2 %product.1 = f32[3,384,256]{2,1,0:T(8,128)} custom-call(f32[3072,1536]{1,0:T(8,128)} %s_ref.1, f32[3,384,256]{2,1,0:T(8,128)} %broadcast_select_fusion.x_ref), custom_call_target="tpu_custom_call" | custom-call | flops 21743271936 | bytes 18874368 | tf_op jit(solution)/shard_map/product/pallas_call | solution.py:408
  156.0 0.0 copy-start.1
  156.0 1.6 negate_select_fusion
  157.6 0.0 copy-done.1
  157.6 0.0 copy-start
  157.6 2.1 %fusion.5 = f32[3,256,256]{2,1,0:T(8,128)S(1)} fusion(f32[3,384,256]{2,1,0:T(8,128)S(1)} %copy-done.1, f32[3,384,256]{2,1,0:T(8,128)S(1)} %negate_select_fusion), kind=kOutput, calls=%fused_computation.19 | convolution fusion | flops 905969664 | bytes 3145728 | tf_op jit(solution)/shard_map/knw,knv->kwv/dot_general | solution.py:443
  159.8 0.0 copy-done
  159.8 0.1 copy.13
  159.8 0.0 copy-start.2
  159.9 0.9 reshape.79.terms
  160.8 41.0 %sum_terms.1 = f32[8,48,128]{2,1,0:T(8,128)} custom-call(f32[4,8,48,128]{3,2,1,0:T(8,128)} %reshape.79.terms), custom_call_target="tpu_custom_call" | custom-call | tf_op jit(solution)/shard_map/sum_terms/pallas_call | solution.py:127
  201.8 1.0 reshape.80
  202.8 0.0 copy-done.2
  202.8 0.7 sub.10
  (3 shorter events, 0.0 us)
Async XLA Ops:
  156.0 1.6 copy-start.1
  157.6 2.2 %copy-start = (f32[3,384,256]{2,1,0:T(8,128)}, f32[3,384,256]{2,1,0:T(8,128)S(1)}, u32[]{:S(2)}) copy-start(f32[3,384,256]{2,1,0:T(8,128)S(1)} %negate_select_fusion) | copy-start | bytes 3538948
  159.8 42.9 %copy-start.2 = (f32[3,64,256]{2,1,0:T(8,128)S(1)}, f32[3,64,256]{2,1,0:T(8,128)}, u32[]{:S(2)}) copy-start(f32[3,64,256]{2,1,0:T(8,128)} %param.7) | copy-start | bytes 589828

commit v4 on v3

--- a/solution.py
+++ b/solution.py
@@ -25,116 +25,98 @@
     return jnp.any(onehot[None] & (table > 0)[:, None, :], axis=2)
 
 
-def sum_kernel(n_row, n_col, terms, out, recv, send1, recv1, send2, recv2):
-    n = n_row * n_col
+def sum_kernel(n_row, n_col, terms, out, swap, half, by_row, line, by_chip, s0, r0, s1, r1, s2, r2, s3, r3):
+    chips = n_col // 2
     row, col = lax.axis_index("row"), lax.axis_index("col")
-    me = row * n_col + col
-
+    chip, core = col // 2, lax.rem(col, 2)
     barrier = pltpu.get_barrier_semaphore()
-
-    def greet(d, carry):
-        other = lax.rem(me + d, n)
+    for d in range(1, n_row):
         pl.semaphore_signal(
-            barrier, inc=1, device_id=(other // n_col, lax.rem(other, n_col)), device_id_type=MESH
-        )
-        return carry
-
-    lax.fori_loop(1, n, greet, 0)
-    pl.semaphore_wait(barrier, n - 1)
-
-    def spread(other):
-        to_row, to_col = other // n_col, lax.rem(other, n_col)
+            barrier, inc=1, device_id=(lax.rem(row + d, n_row), col), device_id_type=MESH
+        )
+    for d in range(1, n_col):
+        pl.semaphore_signal(
+            barrier, inc=1, device_id=(row, lax.rem(col + d, n_col)), device_id_type=MESH
+        )
+    pl.semaphore_wait(barrier, n_row + n_col - 2)
+
+    def remote(src, dst, send, recv, to):
         return pltpu.make_async_remote_copy(
-            src_ref=terms.at[to_row, to_col],
-            dst_ref=recv.at[me],
-            send_sem=send1.at[other],
-            recv_sem=recv1.at[me],
-            device_id=(to_row, to_col),
-            device_id_type=MESH,
-        )
-
-    def arrive(other):
-        return pltpu.make_async_remote_copy(
-            src_ref=terms.at[row, col],
-            dst_ref=recv.at[other],
-            send_sem=send1.at[other],
-            recv_sem=recv1.at[other],
-            device_id=(row, col),
-            device_id_type=MESH,
-        )
-
-    def start1(d, carry):
-        spread(lax.rem(me + d, n)).start()
-        return carry
-
-    lax.fori_loop(1, n, start1, 0)
-
-    def add(d, total):
-        other = lax.rem(me + n - d, n)
-        arrive(other).wait_recv()
-        return total + recv[other]
-
-    total = lax.fori_loop(1, n, add, terms[row, col])
+            src_ref=src, dst_ref=dst, send_sem=send, recv_sem=recv, device_id=to, device_id_type=MESH
+        )
+
+    pair = remote(terms.at[1 - core], swap, s0.at[0], r0.at[0], (row, 2 * chip + 1 - core))
+    pair.start()
+    pair.wait()
+    half[...] = terms[core] + swap[...]
+
+    def to_row(d):
+        other = lax.rem(row + d, n_row)
+        return remote(half.at[other], by_row.at[row], s1.at[other], r1.at[row], (other, col))
+
+    def to_chip(d):
+        other = lax.rem(chip + d, chips)
+        return remote(
+            line.at[other], by_chip.at[chip], s2.at[other], r2.at[chip], (row, 2 * other + core)
+        )
+
+    def to_col(d):
+        other = lax.rem(col + d, n_col)
+        return remote(out.at[col], out.at[col], s3.at[other], r3.at[col], (row, other))
+
+    for d in range(1, n_row):
+        to_row(d).start()
+    line[...] = half[row]
+    for d in range(1, n_row):
+        other = lax.rem(row + n_row - d, n_row)
+        slot = by_row.at[other]
+        remote(slot, slot, s1.at[other], r1.at[other], (row, col)).wait_recv()
+        line[...] += by_row[other]
+    for d in range(1, chips):
+        to_chip(d).start()
+    total = line[chip]
+    for d in range(1, chips):
+        other = lax.rem(chip + chips - d, chips)
+        slot = by_chip.at[other]
+        remote(slot, slot, s2.at[other], r2.at[other], (row, col)).wait_recv()
+        total += by_chip[other]
     out[col] = total
-
-    def share(to_col):
-        return pltpu.make_async_remote_copy(
-            src_ref=out.at[col],
-            dst_ref=out.at[col],
-            send_sem=send2.at[to_col],
-            recv_sem=recv2.at[col],
-            device_id=(row, to_col),
-            device_id_type=MESH,
-        )
-
-    def shared(from_col):
-        return pltpu.make_async_remote_copy(
-            src_ref=out.at[from_col],
-            dst_ref=out.at[from_col],
-            send_sem=send2.at[from_col],
-            recv_sem=recv2.at[from_col],
-            device_id=(row, from_col),
-            device_id_type=MESH,
-        )
-
-    def start2(d, carry):
-        share(lax.rem(col + d, n_col)).start()
-        return carry
-
-    lax.fori_loop(1, n_col, start2, 0)
-
-    def end1(d, carry):
-        spread(lax.rem(me + d, n)).wait_send()
-        return carry
-
-    lax.fori_loop(1, n, end1, 0)
-
-    def end2(d, carry):
-        shared(lax.rem(col + n_col - d, n_col)).wait_recv()
-        share(lax.rem(col + d, n_col)).wait_send()
-        return carry
-
-    lax.fori_loop(1, n_col, end2, 0)
+    for d in range(1, n_col):
+        to_col(d).start()
+    for d in range(1, n_col):
+        other = lax.rem(col + n_col - d, n_col)
+        slot = out.at[other]
+        remote(slot, slot, s3.at[other], r3.at[other], (row, col)).wait_recv()
+    for d in range(1, n_row):
+        to_row(d).wait_send()
+    for d in range(1, chips):
+        to_chip(d).wait_send()
+    for d in range(1, n_col):
+        to_col(d).wait_send()
 
 
 def sum_terms(terms, n_row, n_col):
     members, width, _ = terms.shape
-    n = n_row * n_col
-    lanes = 128
-    depth = members * width * width // (n * lanes)
+    chips, lanes = n_col // 2, 128
+    depth = members * width * width // (n_row * n_col * lanes)
     terms = terms.reshape(members, n_row, width // n_row, width).transpose(1, 0, 2, 3)
-    terms = terms.reshape(n_row, n_col, depth, lanes)
+    terms = terms.reshape(n_row, chips, 2, depth, lanes).transpose(2, 0, 1, 3, 4)
+    f32, sem = jnp.float32, pltpu.SemaphoreType.DMA
     total = pl.pallas_call(
         functools.partial(sum_kernel, n_row, n_col),
-        out_shape=jax.ShapeDtypeStruct((n_col, depth, lanes), jnp.float32),
+        out_shape=jax.ShapeDtypeStruct((n_col, depth, lanes), f32),
         in_specs=[pl.BlockSpec(memory_space=pltpu.VMEM)],
         out_specs=pl.BlockSpec(memory_space=pltpu.VMEM),
         scratch_shapes=[
-            pltpu.VMEM((n, depth, lanes), jnp.float32),
-            pltpu.SemaphoreType.DMA((n,)),
-            pltpu.SemaphoreType.DMA((n,)),
-            pltpu.SemaphoreType.DMA((n_col,)),
-            pltpu.SemaphoreType.DMA((n_col,)),
+            pltpu.VMEM((n_row, chips, depth, lanes), f32),
+            pltpu.VMEM((n_row, chips, depth, lanes), f32),
+            pltpu.VMEM((n_row, chips, depth, lanes), f32),
+            pltpu.VMEM((chips, depth, lanes), f32),
+            pltpu.VMEM((chips, depth, lanes), f32),
+            sem((1,)), sem((1,)),
+            sem((n_row,)), sem((n_row,)),
+            sem((chips,)), sem((chips,)),
+            sem((n_col,)), sem((n_col,)),
         ],
         compiler_params=pltpu.CompilerParams(collective_id=1, has_side_effects=True),
         name="sum_terms",

time: 204 us -> 196 us (0.961)
  Pallas kernels: 192 us -> 184 us
    pallas_call x1, Pallas kernels: 41 us -> 32.5 us  [sum_terms(): pl.pallas_call(functools.partial(sum_kernel, n_row, n_col), out_shape=jax...]
where the time goes in v4:
time: 196 us; the launch traced here: 195 us
  Pallas kernels  184 us (94%)
  other arithmetic  6.46 us (3%)
  matrix products  2.14 us (1%)
  local copies, waits for them, and re-layouts  2.08 us (1%)
    pallas_call x1, Pallas kernels, product(): pl.pallas_call(functools.partial(product_kernel, n_row, n_col), out_shape...  151 us
    pallas_call x1, Pallas kernels, sum_terms(): pl.pallas_call(functools.partial(sum_kernel, n_row, n_col), out_shape=jax...  32.5 us

profile of v4, /device:TPU:0, one launch (start us, length us, event | category | flops | bytes accessed | tf_op | source)
XLA Modules:
  0.0 195.1 jit_solution(6578774689550468718)
XLA Ops:
  0.6 0.7 iota_compare_fusion.2
  1.4 0.8 fusion.1
  2.2 0.1 and_reduce_fusion
  2.3 2.5 %broadcast_select_fusion.x_ref = f32[3,384,256]{2,1,0:T(8,128)} fusion(f32[3,384,256]{2,1,0:T(8,128)} %param.6, pred[3,384]{1,0:T(4,128)(4,1)S(1)} %and_reduce_fusion), kind=kLoop, calls=%fused_computation.3 | loop fusion | flops 294912 | bytes 2360448 | tf_op jit(solution)/shard_map/jit(_where)/select_n | solution.py:423
  4.8 151.2 %product.1 = f32[3,384,256]{2,1,0:T(8,128)} custom-call(f32[3072,1536]{1,0:T(8,128)} %s_ref.1, f32[3,384,256]{2,1,0:T(8,128)} %broadcast_select_fusion.x_ref), custom_call_target="tpu_custom_call" | custom-call | flops 21743271936 | bytes 18874368 | tf_op jit(solution)/shard_map/product/pallas_call | solution.py:390
  156.0 0.0 copy-start.1
  156.0 1.6 negate_select_fusion
  157.6 0.0 copy-done.1
  157.6 0.0 copy-start
  157.6 2.1 %fusion.5 = f32[3,256,256]{2,1,0:T(8,128)S(1)} fusion(f32[3,384,256]{2,1,0:T(8,128)S(1)} %copy-done.1, f32[3,384,256]{2,1,0:T(8,128)S(1)} %negate_select_fusion), kind=kOutput, calls=%fused_computation.20 | convolution fusion | flops 905969664 | bytes 3145728 | tf_op jit(solution)/shard_map/knw,knv->kwv/dot_general | solution.py:425
  159.8 0.0 copy-done
  159.8 0.1 copy.18
  159.8 0.1 reshape.79
  159.9 0.0 copy-start.2
  159.9 0.9 copy.17
  160.9 32.5 %sum_terms.1 = f32[8,48,128]{2,1,0:T(8,128)} custom-call(f32[2,4,4,48,128]{4,3,2,1,0:T(8,128)} %bitcast.13), custom_call_target="tpu_custom_call" | custom-call | tf_op jit(solution)/shard_map/sum_terms/pallas_call | solution.py:105
  193.4 1.0 reshape.80
  194.4 0.0 copy-done.2
  194.4 0.7 sub.10
  (3 shorter events, 0.0 us)
Async XLA Ops:
  156.0 1.6 copy-start.1
  157.6 2.2 %copy-start = (f32[3,384,256]{2,1,0:T(8,128)}, f32[3,384,256]{2,1,0:T(8,128)S(1)}, u32[]{:S(2)}) copy-start(f32[3,384,256]{2,1,0:T(8,128)S(1)} %negate_select_fusion) | copy-start | bytes 3538948
  159.9 34.5 %copy-start.2 = (f32[3,64,256]{2,1,0:T(8,128)S(1)}, f32[3,64,256]{2,1,0:T(8,128)}, u32[]{:S(2)}) copy-start(f32[3,64,256]{2,1,0:T(8,128)} %param.7) | copy-start | bytes 589828
